TPU v7x, 32 devices: a whole 2x2x4 slice. The times are simulated.
32 devices in a mesh: layer: 8 (over y, x, core), dp: 4 (over z).
Axes of the slice: x: 2, y: 2, z: 4, core: 2. Of those that a mesh axis runs over, the one named last changes fastest.
Arguments:
- states_guess: float32 [8, 4, 32, 32, 128], P('layer', 'dp'), may hold values from -6 to 6
- kernels: bfloat16 [8, 9, 128, 128], P('layer'), may hold values from -0.1875 to 0.1875
- adjoint_end: float32 [8, 4, 32, 32, 128], P('layer', 'dp'), may hold values from -6 to 6
- coarse_gain: float32 [8, 128], replicated, may hold values from 0 to 1
Outputs:
- new_states: float32 [8, 4, 32, 32, 128], P('layer', 'dp')
- adjoint_start: float32 [8, 4, 32, 32, 128], P('layer', 'dp')
- weight_grad: float32 [8, 9, 128, 128], P('layer')
- relax_change: float32 [8, 4, 32, 32, 128], P('layer', 'dp')
- adjoint_change: float32 [8, 4, 32, 32, 128], P('layer', 'dp')
All inputs are finite; a program needn't handle non-finite values.
Results may differ from a plain program's by a relative error of at most 0.0048.
Values sent between devices are 32-bit elements; how exact they have to be, the bound alone decides.
A program may use at most 64 MiB of HBM per device.

v0:
```python
import jax
import jax.numpy as jnp
from jax import lax
from jax.sharding import PartitionSpec as P

EPSILON = 1e-06


def shifted(block, axis, distance):
    devices = range(lax.axis_size(axis))
    route = [(i - distance, i) for i in devices if i - distance in devices]
    return lax.ppermute(block, axis, route)


def stacked_windows(source, flipped):
    images, height, across, channels = source.shape
    padded = jnp.pad(source, ((0, 0), (1, 1), (1, 1), (0, 0)))
    windows = []
    for stencil in range(9):
        if flipped:
            row_start = 2 - stencil // 3
            col_start = 2 - stencil % 3
        else:
            row_start = stencil // 3
            col_start = stencil % 3
        windows.append(padded[:, row_start : row_start + height, col_start : col_start + across, :])
    return jnp.concatenate(windows, axis=3).reshape(images * height * across, 9 * channels)


def conv_apply(source, kernel_set):
    images, height, across, channels = source.shape
    columns = stacked_windows(source, False)
    summed = jnp.dot(
        columns, kernel_set.reshape(9 * channels, channels), preferred_element_type=jnp.float32
    )
    return summed.reshape(images, height, across, channels)


def conv_back(source, kernel_set):
    images, height, across, channels = source.shape
    columns = stacked_windows(source, True)
    turned = jnp.transpose(kernel_set, (0, 2, 1)).reshape(9 * channels, channels)
    summed = jnp.dot(columns, turned, preferred_element_type=jnp.float32)
    return summed.reshape(images, height, across, channels)


def conv_weight(source, weighted):
    images, height, across, channels = source.shape
    columns = stacked_windows(source, False)
    flat_error = weighted.reshape(-1, channels)
    result = lax.dot_general(
        columns, flat_error, (((0,), (0,)), ((), ())), preferred_element_type=jnp.float32
    )
    return result.reshape(9, channels, channels)


def step_length(layer_pos, layers):
    return (1.0 + 2.0 * layer_pos / (layers - 1)) / layers


def forward_block(start_state, kernel_set, first_layer, layers):
    current = start_state
    step_len = step_length((first_layer + 0).astype(jnp.float32), layers)
    current = current + step_len * jnp.tanh(conv_apply(current.astype(jnp.bfloat16), kernel_set[0]))
    return current


def record_block(start_state, kernel_set):
    rounded = start_state.astype(jnp.bfloat16)
    activation = jnp.tanh(conv_apply(rounded, kernel_set[0]))
    stored = [rounded]
    slopes = [1.0 - activation * activation]
    return (stored, slopes)


def backward_block(end_state, stored, slopes, kernel_set, first_layer, layers, with_gradient):
    adjoint = end_state
    gradients = []
    for local_pos in reversed(range(kernel_set.shape[0])):
        step_len = step_length((first_layer + local_pos).astype(jnp.float32), layers)
        weighted = (adjoint * slopes[local_pos]).astype(jnp.bfloat16)
        if with_gradient:
            gradients.insert(0, step_len * conv_weight(stored[local_pos], weighted))
        adjoint = adjoint + step_len * conv_back(weighted, kernel_set[local_pos])
    if with_gradient:
        return (adjoint, jnp.stack(gradients))
    return adjoint


def local(states_guess, kernels, adjoint_end, coarse_gain):
    blocks = lax.axis_size("layer")
    local_layers = kernels.shape[0]
    layers = local_layers * blocks
    channels = kernels.shape[3]
    position = lax.axis_index("layer")
    first_layer = position * local_layers
    is_first = position == 0
    is_last = position == blocks - 1
    anchor = states_guess[0]
    block_gain = lax.dynamic_slice_in_dim(coarse_gain, position, 1, 0)[0]
    first_ends = forward_block(anchor, kernels, first_layer, layers)
    first_starts = jnp.where(is_first, anchor, shifted(first_ends, "layer", 1))
    second_ends = forward_block(first_starts, kernels, first_layer, layers)
    second_starts = jnp.where(is_first, anchor, shifted(second_ends, "layer", 1))
    third_ends = forward_block(second_starts, kernels, first_layer, layers)
    relax_change = third_ends - second_ends
    offsets = third_ends - block_gain * second_starts
    coarse_terms = jnp.where(is_first, third_ends, offsets)
    rows_per_block = jnp.arange(blocks, dtype=jnp.int32)
    mask_between = (rows_per_block[None, :] > rows_per_block[:, None]) & (
        rows_per_block[None, :] < position
    )
    factors = jnp.prod(
        jnp.where(mask_between[:, :, None], coarse_gain[None, :, :], jnp.float32(1.0)), axis=1
    )
    weights = jnp.where((rows_per_block < position)[:, None], factors, jnp.float32(0.0))
    folded = jnp.sum(
        weights[:, None, None, None, :]
        * lax.all_gather(coarse_terms[None], "layer", axis=0, tiled=True),
        axis=0,
    )
    corrected = jnp.where(is_first, anchor, folded)
    stored, slopes = record_block(corrected, kernels)
    final_end = adjoint_end[0]
    first_back = backward_block(final_end, stored, slopes, kernels, first_layer, layers, False)
    adjoint_mid = jnp.where(is_last, final_end, shifted(first_back, "layer", -1))
    second_back = backward_block(adjoint_mid, stored, slopes, kernels, first_layer, layers, False)
    adjoint_last = jnp.where(is_last, final_end, shifted(second_back, "layer", -1))
    adjoint_start, gradients = backward_block(
        adjoint_last, stored, slopes, kernels, first_layer, layers, True
    )
    adjoint_change = adjoint_start - second_back
    entry_count = layers * 9 * channels * channels
    summed_grad = lax.psum(gradients, "dp")
    squares = lax.psum(jnp.sum(summed_grad * summed_grad), "layer")
    weight_grad = summed_grad / jnp.sqrt(squares / entry_count + EPSILON)
    return (
        corrected[None],
        adjoint_start[None],
        weight_grad,
        relax_change[None],
        adjoint_change[None],
    )


def solution(mesh):
    in_specs = (
        P("layer", "dp", None, None, None),
        P("layer", None, None, None),
        P("layer", "dp", None, None, None),
        P(),
    )
    out_specs = (
        P("layer", "dp", None, None, None),
        P("layer", "dp", None, None, None),
        P("layer", None, None, None),
        P("layer", "dp", None, None, None),
        P("layer", "dp", None, None, None),
    )
    return jax.shard_map(local, mesh=mesh, in_specs=in_specs, out_specs=out_specs, check_vma=False)
```

profile of v0, /device:TPU:0, one launch (start us, length us, event | category | flops | bytes accessed | tf_op | source)
XLA Modules:
  0.0 187.3 jit_solution(6792553646967941074)
XLA Ops:
  7.2 1.1 bitcast_convert_fusion.1
  8.4 0.8 fusion.66
  9.9 0.8 fusion.70
  10.7 0.8 fusion.72
  11.5 0.8 fusion.130
  12.3 0.8 fusion.74
  13.1 0.8 fusion.76
  13.9 0.8 fusion.78
  14.6 0.8 fusion.80
  15.4 2.4 %fusion.19 = f32[1,32,32,128]{3,2,1,0:T(8,128)S(1)} fusion(bf16[32,32,1152]{2,1,0:T(8,128)(2,1)} %fusion.80, bf16[1152,128,1]{1,0,2:T(8,128)(2,1)S(1)} %bitcast.258, f32[1,1,32,32,128]{4,3,2,1,0:T(8,128)S(1)} %copy-done, f32[]{:T(128)S(6)} %div.11), kind=kOutput, calls=%fused_computation.19 | convolution fusion | flops 302252032 | bytes 3702788 | tf_op jit(solution)/shard_map/dot_general | solution.py:33
  17.9 2.4 %collective-permute-start = (f32[1,32,32,128]{3,2,1,0:T(8,128)S(1)}, f32[1,32,32,128]{3,2,1,0:T(8,128)S(1)}, u32[]{:S(2)}, u32[]{:S(2)}) collective-permute-start(f32[1,32,32,128]{3,2,1,0:T(8,128)S(1)} %fusion.19), channel_id=1, source_target_pairs={{0,4},{4,8},{8,12},{12,16},{16,20},{20,24},{24,28},{1,5},{5,9},{9,... | collective-permute-start | bytes 1572872 | tf_op jit(solution)/shard_map/ppermute | solution.py:12
  20.3 1.5 collective-permute-done
  22.7 0.8 fusion.53
  23.5 9.1 %collective-permute-start.1 = (f32[1,32,32,128]{3,2,1,0:T(8,128)S(1)}, f32[1,32,32,128]{3,2,1,0:T(8,128)S(1)}, u32[]{:S(2)}, u32[]{:S(2)}) collective-permute-start(f32[1,32,32,128]{3,2,1,0:T(8,128)S(1)} %fusion.53), channel_id=1, source_target_pairs={{0,4},{4,8},{8,12},{12,16},{16,20},{20,24},{24,28},{1,5},{5,9},{9,... | collective-permute-start | bytes 1572872 | tf_op jit(solution)/shard_map/ppermute | solution.py:12
  32.7 1.5 collective-permute-done.1
  35.1 1.8 subtract_bitcast_fusion.1
  37.4 46.5 %all-gather.3.cloned.1.call-done = f32[8,32,32,128]{3,2,1,0:T(8,128)} async-done(((f32[1,32,32,128]{3,2,1,0:T(8,128)}), f32[8,32,32,128]{3,2,1,0:T(8,128)}) %all-gather.3.cloned.1.call-update) | async-done | bytes 4194320 | tf_op jit(solution)/shard_map/all_gather | solution.py:119
  83.8 2.8 %fusion = f32[32,32,128]{2,1,0:T(8,128)S(1)} fusion(f32[8,32,32,128]{3,2,1,0:T(8,128)} %all-gather.3.cloned.1.call-done, f32[8,128]{1,0:T(8,128)S(1)} %broadcast_select_fusion), kind=kLoop, calls=%fused_computation.1 | loop fusion | flops 1966080 | bytes 4722688 | tf_op jit(solution)/shard_map/reduce_sum | solution.py:117
  88.2 0.8 fusion.63
  89.9 0.8 fusion.46
  90.7 1.3 collective-permute-start.2
  92.7 0.7 constant_dynamic-update-slice_fusion.12
  93.5 0.8 constant_dynamic-update-slice_fusion.11
  95.0 0.8 constant_dynamic-update-slice_fusion.9
  95.8 0.8 constant_dynamic-update-slice_fusion.8
  97.6 0.8 fusion.50
  98.4 1.5 collective-permute-start.3
  99.9 0.8 constant_dynamic-update-slice_fusion.7
  100.6 0.8 constant_dynamic-update-slice_fusion.6
  102.1 4.3 %copy.15 = bf16[1152,1024]{1,0:T(8,128)(2,1)} copy(bf16[1152,1024]{0,1:T(8,128)(2,1)} %bitcast.65) | data formatting | bytes 4718592 | tf_op jit(solution)/shard_map/dot_general | solution.py:51
  106.4 0.9 bitcast_select_fusion.4
  107.3 1.3 fusion.61
  108.6 0.8 fusion.121
  109.4 0.7 fusion.122
  110.2 0.8 fusion.123
  111.0 0.8 fusion.124
  111.8 0.8 constant_dynamic-update-slice_fusion.4
  112.6 0.8 fusion.125
  113.4 1.6 fusion.9
  115.0 0.8 fusion.126
  115.8 0.8 fusion.127
  116.6 0.8 fusion.128
  117.4 2.5 %fusion.47 = f32[1,32,32,128]{3,2,1,0:T(8,128)S(1)} fusion(bf16[1152,128,1]{1,0,2:T(8,128)(2,1)S(1)} %bitcast.264, bf16[1,32,32,1152]{3,2,1,0:T(8,128)(2,1)} %fusion.128, f32[]{:T(128)S(6)} %div.11, f32[1,32,32,128]{3,2,1,0:T(8,128)} %collective-permute-done.3, f32[1,1,32,32,128]{4,3,2,1,0:T(8,128)S(1)} %copy-done.1, pred[]{:T(512)S(6)} %eq.7), kind=kOutput, calls=%fused_computation.32 | convolution fusion | flops 302383104 | bytes 4227077 | tf_op jit(solution)/shard_map/dot_general | solution.py:43
  119.9 42.4 %all-reduce.9.cloned.1.call-done = f32[1,9,128,128]{3,2,1,0:T(8,128)} async-done(((f32[1,9,128,128]{3,2,1,0:T(8,128)}), f32[1,9,128,128]{3,2,1,0:T(8,128)}) %all-reduce.9.cloned.1.call-update) | async-done | bytes 589840 | tf_op jit(solution)/shard_map/psum | solution.py:134
  162.3 1.9 %multiply_reduce_fusion = f32[]{:T(128)} fusion(f32[1,9,128,128]{3,2,1,0:T(8,128)} %all-reduce.9.cloned.1.call-done), kind=kLoop, calls=%fused_computation.37 | loop fusion | flops 294911 | bytes 589828 | tf_op jit(solution)/shard_map/reduce_sum | solution.py:135
  164.2 0.9 subtract_bitcast_fusion
  165.1 13.8 %psum.15 = f32[]{:T(128)} all-reduce(f32[]{:T(128)} %multiply_reduce_fusion), channel_id=1, replica_groups=mesh['layer'=8,'dp'=4] {'layer'}, use_global_device_ids=true, to_apply=%region_4.5 | all-reduce | flops 1 | bytes 8 | tf_op jit(solution)/shard_map/psum | solution.py:135
  179.6 0.9 broadcast_divide_fusion
  (80 shorter events, 8.6 us)
Async XLA Ops:
  7.2 4.3 %copy-start = (f32[1,1,32,32,128]{4,3,2,1,0:T(8,128)S(1)}, f32[1,1,32,32,128]{4,3,2,1,0:T(8,128)}, u32[]{:S(2)}) copy-start(f32[1,1,32,32,128]{4,3,2,1,0:T(8,128)} %param.4) | copy-start | bytes 1572868
  7.2 76.7 %all-gather.3.cloned.1.call-start = ((), (), s32[]{:S(2)}) async-start(), calls=%async_computation.1 | async-start | bytes 4718592 | tf_op jit(solution)/shard_map/all_gather | solution.py:119
  9.2 6.3 %copy-start.3 = (bf16[1,9,128,128]{3,2,1,0:T(8,128)(2,1)S(1)}, bf16[1,9,128,128]{3,2,1,0:T(8,128)(2,1)}, u32[]{:S(2)}) copy-start(bf16[1,9,128,128]{3,2,1,0:T(8,128)(2,1)} %param.5) | copy-start | bytes 884740
  17.9 3.9 %collective-permute-start = (f32[1,32,32,128]{3,2,1,0:T(8,128)S(1)}, f32[1,32,32,128]{3,2,1,0:T(8,128)S(1)}, u32[]{:S(2)}, u32[]{:S(2)}) collective-permute-start(f32[1,32,32,128]{3,2,1,0:T(8,128)S(1)} %fusion.19), channel_id=1, source_target_pairs={{0,4},{4,8},{8,12},{12,16},{16,20},{20,24},{24,28},{1,5},{5,9},{9,... | collective-permute-start | bytes 1572872 | tf_op jit(solution)/shard_map/ppermute | solution.py:12
  22.6 10.1 %copy-start.6 = (f32[8,128]{1,0:T(8,128)S(1)}, f32[8,128]{1,0:T(8,128)}, u32[]{:S(2)}) copy-start(f32[8,128]{1,0:T(8,128)} %param.7) | copy-start | bytes 12292
  23.5 10.6 %collective-permute-start.1 = (f32[1,32,32,128]{3,2,1,0:T(8,128)S(1)}, f32[1,32,32,128]{3,2,1,0:T(8,128)S(1)}, u32[]{:S(2)}, u32[]{:S(2)}) collective-permute-start(f32[1,32,32,128]{3,2,1,0:T(8,128)S(1)} %fusion.53), channel_id=1, source_target_pairs={{0,4},{4,8},{8,12},{12,16},{16,20},{20,24},{24,28},{1,5},{5,9},{9,... | collective-permute-start | bytes 1572872 | tf_op jit(solution)/shard_map/ppermute | solution.py:12
  36.9 125.4 %all-reduce.9.cloned.1.call-start = ((), (), s32[]{:S(2)}) async-start(), calls=%async_computation | async-start | bytes 1179648 | tf_op jit(solution)/shard_map/psum | solution.py:134
  87.2 1.0 copy-start.1
  90.7 5.9 %collective-permute-start.2 = (f32[1,32,32,128]{3,2,1,0:T(8,128)S(1)}, f32[1,32,32,128]{3,2,1,0:T(8,128)S(1)}, u32[]{:S(2)}, u32[]{:S(2)}) collective-permute-start(f32[1,32,32,128]{3,2,1,0:T(8,128)S(1)} %fusion.46), channel_id=1, source_target_pairs={{4,0},{8,4},{12,8},{16,12},{20,16},{24,20},{28,24},{5,1},{9,5},{13... | collective-permute-start | bytes 1572872 | tf_op jit(solution)/shard_map/ppermute | solution.py:12
  98.4 8.9 %collective-permute-start.3 = (f32[1,32,32,128]{3,2,1,0:T(8,128)S(1)}, f32[1,32,32,128]{3,2,1,0:T(8,128)}, u32[]{:S(2)}, u32[]{:S(2)}) collective-permute-start(f32[1,32,32,128]{3,2,1,0:T(8,128)S(1)} %fusion.50), channel_id=1, source_target_pairs={{4,0},{8,4},{12,8},{16,12},{20,16},{24,20},{28,24},{5,1},{9,5},{13... | collective-permute-start | bytes 1572872 | tf_op jit(solution)/shard_map/ppermute | solution.py:12
  107.3 6.1 %copy-start.2 = (bf16[1152,1024]{1,0:T(8,128)(2,1)S(1)}, bf16[1152,1024]{1,0:T(8,128)(2,1)}, u32[]{:S(2)}) copy-start(bf16[1152,1024]{1,0:T(8,128)(2,1)} %copy.15) | copy-start | bytes 7077892
  119.9 60.5 %copy-start.5 = (f32[1,32,32,128]{3,2,1,0:T(8,128)}, f32[1,32,32,128]{3,2,1,0:T(8,128)S(1)}, u32[]{:S(2)}) copy-start(f32[1,32,32,128]{3,2,1,0:T(8,128)S(1)} %fusion.47) | copy-start | bytes 1572868
  162.3 17.2 %copy-start.4 = (f32[1,9,128,128]{3,2,1,0:T(8,128)S(1)}, f32[1,9,128,128]{3,2,1,0:T(8,128)}, u32[]{:S(2)}) copy-start(f32[1,9,128,128]{3,2,1,0:T(8,128)} %all-reduce.9.cloned.1.call-done) | copy-start | bytes 1769476
Sparse Core Ops, SparseCore 0:
  37.0 46.7 all-gather.2
  115.1 47.1 all-reduce.8
where the time goes:
time: 188 us; the launch traced here: 187 us
  waiting for transfers between devices  91.8 us (49%)
  local copies, waits for them, and re-layouts  28.6 us (15%)
  between operations  15.2 us (8%)
  starting transfers between devices  14.4 us (8%)
  blocking collectives  13.8 us (7%)
  other arithmetic  12.1 us (6%)
  matrix products  11.5 us (6%)
    all_gather x1, waiting for transfers between devices, local(): lax.all_gather(coarse_terms[None], 'layer', axis=0, tiled=True)  46.5 us
    psum x1, waiting for transfers between devices, local(): summed_grad = lax.psum(gradients, 'dp')  42.4 us
    unnamed x76, local copies, waits for them, and re-layouts  21.1 us
    ppermute x4, starting transfers between devices, shifted(): return lax.ppermute(block, axis, route)  14.3 us
    psum x1, blocking collectives, local(): squares = lax.psum(jnp.sum(summed_grad * summed_grad), 'layer')  13.8 us
    dot_general x4, matrix products, conv_apply(): jnp.dot(columns, kernel_set.reshape(9 * channels, channels), preferred_el...  5.81 us
    dot_general x1, local copies, waits for them, and re-layouts, conv_weight(): lax.dot_general(columns, flat_error, (((0,), (0,)), ((), ())), preferred_...  4.28 us
    dot_general x3, matrix products, conv_back(): summed = jnp.dot(columns, turned, preferred_element_type=jnp.float32)  4.09 us
  transfers between devices with their start and end apart: 6, of which 4 were waited for; matrix products, arithmetic and copies ran while one was open for 9% of the time, Pallas kernels for 0%

commit v1 on v0

v1 whole, which is shorter than its diff:
```python
import functools

import jax
import jax.numpy as jnp
from jax import lax
from jax.experimental import pallas as pl
from jax.experimental.pallas import tpu as pltpu
from jax.sharding import PartitionSpec as P

EPSILON = 1e-06
CHUNKS = 4
LAG = 2


def kernel(
    L, Z, side, anchor, kern, aend, gain,
    ns, ast, gsum, sqsum, rc, ac,
    tx, rx, off, xcf, xcd, slopes, xt, wb, gacc, gout_rx, gin_rx, sqrx, sqtx,
    send_sem, recv_sem, gsend_in, grecv_out, gsend_out, grecv_in, sq_send, sq_recv,
):
    n, ch = anchor.shape
    nc = CHUNKS
    R = n // nc
    pos = lax.axis_index("layer")
    zp = lax.axis_index("dp")
    is_first, is_last = pos == 0, pos == L - 1
    not_first, not_last = pos > 0, pos < L - 1
    half = Z // 2
    on_left = zp < half
    inward = jnp.where(on_left, zp + 1, zp - 1)
    has_out = (zp > 0) & (zp < Z - 1)
    no_out = (zp == 0) | (zp == Z - 1)
    outward = jnp.where(no_out, zp, jnp.where(on_left, zp - 1, zp + 1))
    is_mid = (zp == half - 1) | (zp == half)
    not_mid = (zp < half - 1) | (zp > half)
    h = (1.0 + 2.0 * pos.astype(jnp.float32) / (L - 1)) / L

    barrier = pltpu.get_barrier_semaphore()
    for k in range(1, L):
        pl.semaphore_signal(
            barrier, inc=1, device_id={"layer": lax.rem(pos + k, L)},
            device_id_type=pl.DeviceIdType.MESH,
        )
    pl.semaphore_signal(barrier, inc=1, device_id={"dp": inward}, device_id_type=pl.DeviceIdType.MESH)

    @pl.when(has_out)
    def _():
        pl.semaphore_signal(barrier, inc=1, device_id={"dp": outward}, device_id_type=pl.DeviceIdType.MESH)

    def rows(c):
        return pl.ds(c * R, R)

    def link(phase, c, dst):
        return pltpu.make_async_remote_copy(
            src_ref=tx.at[phase, rows(c)],
            dst_ref=rx.at[phase, rows(c)],
            send_sem=send_sem.at[phase, c],
            recv_sem=recv_sem.at[phase, c],
            device_id={"layer": dst},
            device_id_type=pl.DeviceIdType.MESH,
        )

    up = lax.rem(pos + 1, L)
    down = lax.rem(pos + L - 1, L)

    def send(phase, c):
        if phase < 3:
            pl.when(not_last)(lambda: link(phase, c, up).start())
        else:
            pl.when(not_first)(lambda: link(phase, c, down).start())

    def arrive(phase, c):
        if phase < 3:
            pl.when(not_first)(lambda: link(phase, c, up).wait_recv())
        else:
            pl.when(not_last)(lambda: link(phase, c, down).wait_recv())

    def sent(phase, c):
        if phase < 3:
            pl.when(not_last)(lambda: link(phase, c, up).wait_send())
        else:
            pl.when(not_first)(lambda: link(phase, c, down).wait_send())

    across = lax.broadcasted_iota(jnp.int32, (R, ch), 0) % side
    left_ok = across > 0
    right_ok = across < side - 1

    def stage(xc, c, value):
        at = pl.ds(side + c * R, R)
        xc[at, 0:ch] = jnp.where(left_ok, pltpu.roll(value, 1, 0), 0.0).astype(jnp.bfloat16)
        xc[at, ch : 2 * ch] = value.astype(jnp.bfloat16)
        xc[at, 2 * ch : 3 * ch] = jnp.where(right_ok, pltpu.roll(value, R - 1, 0), 0.0).astype(jnp.bfloat16)

    def conv(xc, w, c):
        total = None
        for d in range(3):
            term = jnp.dot(
                xc[pl.ds(c * R + side * d, R), :], w[d], preferred_element_type=jnp.float32
            )
            total = term if total is None else total + term
        return total

    zeros = jnp.zeros((side, 3 * ch), jnp.bfloat16)
    for xc in (xcf, xcd):
        xc[0:side, :] = zeros
        xc[n + side : n + 2 * side, :] = zeros

    for c in range(nc):
        stage(xcf, c, anchor[rows(c), :])
    for c in range(nc):
        tx[0, rows(c), :] = anchor[rows(c), :] + h * jnp.tanh(conv(xcf, kern, c))
        if c == 0:
            pl.semaphore_wait(barrier, jnp.where(has_out, L + 1, L))
        send(0, c)

    @pl.when(is_first)
    def _():
        for p in range(3):
            rx[p] = anchor[...]

    @pl.when(is_last)
    def _():
        for p in range(3, 5):
            rx[p] = aend[...]

    for d in range(3):
        for e in range(3):
            tap = kern[2 - d, (2 - e) * ch : (3 - e) * ch, :]
            wb[d, e * ch : (e + 1) * ch, :] = tap.astype(jnp.float32).T.astype(jnp.bfloat16)

    block_gain = gain[pl.ds(pos, 1), :]

    def second(c):
        tx[1, rows(c), :] = rx[0, rows(c), :] + h * jnp.tanh(conv(xcf, kern, c))
        send(1, c)

    for c in range(nc):
        arrive(0, c)
        stage(xcf, c, rx[0, rows(c), :])
        if c > 0:
            second(c - 1)
    second(nc - 1)

    def third(c):
        start = rx[1, rows(c), :]
        end = start + h * jnp.tanh(conv(xcf, kern, c))
        rc[rows(c), :] = end - tx[1, rows(c), :]
        off[rows(c), :] = end - block_gain * start

    for c in range(nc):
        arrive(1, c)
        stage(xcf, c, rx[1, rows(c), :])
        if c > 0:
            third(c - 1)
    third(nc - 1)

    def record(c):
        act = jnp.tanh(conv(xcf, kern, c))
        slopes[rows(c), :] = 1.0 - act * act
        xt[:, rows(c)] = xcf[pl.ds(side + c * R, R), :].T

    for c in range(nc):
        arrive(2, c)
        state = rx[2, rows(c), :]
        tx[2, rows(c), :] = block_gain * state + off[rows(c), :]
        send(2, c)
        ns[rows(c), :] = state
        stage(xcf, c, state)
        if c > 0:
            record(c - 1)
    record(nc - 1)

    for c in range(nc):
        stage(xcd, c, aend[rows(c), :] * slopes[rows(c), :])
    for c in range(nc):
        tx[3, rows(c), :] = aend[rows(c), :] + h * conv(xcd, wb, c)
        send(3, c)

    def second_back(c):
        tx[4, rows(c), :] = rx[3, rows(c), :] + h * conv(xcd, wb, c)
        send(4, c)

    for c in range(nc):
        arrive(3, c)
        stage(xcd, c, rx[3, rows(c), :] * slopes[rows(c), :])
        if c > 0:
            second_back(c - 1)
    second_back(nc - 1)

    for c in range(nc):
        arrive(4, c)
        stage(xcd, c, rx[4, rows(c), :] * slopes[rows(c), :])

    def g_in(t, dst):
        return pltpu.make_async_remote_copy(
            src_ref=gacc.at[t], dst_ref=dst.at[t], send_sem=gsend_in.at[t],
            recv_sem=(grecv_out if dst is gout_rx else grecv_in).at[t],
            device_id={"dp": inward}, device_id_type=pl.DeviceIdType.MESH,
        )

    def g_out(t):
        return pltpu.make_async_remote_copy(
            src_ref=gsum.at[t], dst_ref=gin_rx.at[t], send_sem=gsend_out.at[t],
            recv_sem=grecv_in.at[t], device_id={"dp": outward},
            device_id_type=pl.DeviceIdType.MESH,
        )

    def push(t):
        pl.when(is_mid)(lambda: g_in(t, gin_rx).start())
        pl.when(not_mid)(lambda: g_in(t, gout_rx).start())

    for d in range(3):
        three = h * jnp.dot(
            xt[...], xcd[pl.ds((2 - d) * side, n), ch : 2 * ch], preferred_element_type=jnp.float32
        )
        for e in range(3):
            gacc[3 * d + e] = three[e * ch : (e + 1) * ch, :]

            @pl.when(no_out)
            def _(t=3 * d + e):
                push(t)

    def towards(t):
        @pl.when(has_out)
        def _():
            g_in(t, gout_rx).wait_recv()
            gacc[t] = gacc[t] + gout_rx[t]
            push(t)

    def outwards(t):
        g_in(t, gin_rx).wait_recv()

        @pl.when(is_mid)
        def _():
            gsum[t] = gacc[t] + gin_rx[t]

        @pl.when(not_mid)
        def _():
            gsum[t] = gin_rx[t]

        pl.when(has_out)(lambda: g_out(t).start())

    def finish(c):
        done = rx[4, rows(c), :] + h * conv(xcd, wb, c)
        ast[rows(c), :] = done
        ac[rows(c), :] = done - tx[4, rows(c), :]

    squares = jnp.zeros((8, ch), jnp.float32)
    for t in range(9 + LAG):
        if t < 9:
            towards(t)
        if t < nc:
            finish(t)
        if t >= LAG:
            outwards(t - LAG)
            block = gsum[t - LAG]
            squares = squares + jnp.sum((block * block).reshape(ch // 8, 8, ch), axis=0)

    sqtx[...] = squares

    def sq(k):
        return pltpu.make_async_remote_copy(
            src_ref=sqtx, dst_ref=sqrx.at[k - 1], send_sem=sq_send.at[k - 1],
            recv_sem=sq_recv.at[k - 1], device_id={"layer": lax.rem(pos + k, L)},
            device_id_type=pl.DeviceIdType.MESH,
        )

    for k in range(1, L):
        sq(k).start()
    for p in range(5):
        for c in range(nc):
            sent(p, c)
    for t in range(9):
        g_in(t, gin_rx).wait_send()
        pl.when(has_out)(lambda t=t: g_out(t).wait_send())
    for k in range(1, L):
        sq(k).wait_recv()
        squares = squares + sqrx[k - 1]
    sqsum[...] = squares
    for k in range(1, L):
        sq(k).wait_send()


def local(L, Z, states_guess, kernels, adjoint_end, coarse_gain):
    side, ch = states_guess.shape[2], states_guess.shape[4]
    images = states_guess.shape[1]
    n = images * side * side
    f32, bf16 = jnp.float32, jnp.bfloat16
    state = jax.ShapeDtypeStruct((n, ch), f32)
    vm = pl.BlockSpec(memory_space=pltpu.VMEM)
    V = pltpu.VMEM
    D = pltpu.SemaphoreType.DMA
    ns, ast, gsum, sq, rc, ac = pl.pallas_call(
        functools.partial(kernel, L, Z, side),
        out_shape=(
            state, state, jax.ShapeDtypeStruct((9, ch, ch), f32),
            jax.ShapeDtypeStruct((8, ch), f32), state, state,
        ),
        in_specs=[vm] * 4,
        out_specs=(vm,) * 6,
        scratch_shapes=[
            V((5, n, ch), f32), V((5, n, ch), f32), V((n, ch), f32),
            V((n + 2 * side, 3 * ch), bf16), V((n + 2 * side, 3 * ch), bf16),
            V((n, ch), f32), V((3 * ch, n), bf16), V((3, 3 * ch, ch), bf16),
            V((9, ch, ch), f32), V((9, ch, ch), f32), V((9, ch, ch), f32),
            V((L - 1, 8, ch), f32), V((8, ch), f32),
            D((5, CHUNKS)), D((5, CHUNKS)), D((9,)), D((9,)), D((9,)), D((9,)),
            D((L - 1,)), D((L - 1,)),
        ],
        compiler_params=pltpu.CompilerParams(
            collective_id=0, has_side_effects=True, vmem_limit_bytes=48 * 1024 * 1024
        ),
    )(
        states_guess.reshape(n, ch), kernels.reshape(3, 3 * ch, ch),
        adjoint_end.reshape(n, ch), coarse_gain,
    )
    weight_grad = gsum / jnp.sqrt(jnp.sum(sq) / (L * 9 * ch * ch) + EPSILON)
    full = states_guess.shape
    return (
        ns.reshape(full), ast.reshape(full), weight_grad.reshape(1, 9, ch, ch),
        rc.reshape(full), ac.reshape(full),
    )


def solution(mesh):
    in_specs = (
        P("layer", "dp", None, None, None),
        P("layer", None, None, None),
        P("layer", "dp", None, None, None),
        P(),
    )
    out_specs = (
        P("layer", "dp", None, None, None),
        P("layer", "dp", None, None, None),
        P("layer", None, None, None),
        P("layer", "dp", None, None, None),
        P("layer", "dp", None, None, None),
    )
    fn = functools.partial(local, mesh.shape["layer"], mesh.shape["dp"])
    return jax.shard_map(fn, mesh=mesh, in_specs=in_specs, out_specs=out_specs, check_vma=False)
```

time: 188 us -> 83 us (0.44)
  waiting for transfers between devices: 91.8 us -> 0 us
  Pallas kernels: 0 us -> 73 us
  local copies, waits for them, and re-layouts: 28.6 us -> 6.89 us
  starting transfers between devices: 14.4 us -> 0 us
  between operations: 15.2 us -> 1.35 us
  blocking collectives: 13.8 us -> 0 us
  matrix products: 11.5 us -> 0 us
  other arithmetic: 12.1 us -> 1.47 us
    pallas_call x0 -> x1, Pallas kernels: none -> 73 us  [local(): pl.pallas_call(functools.partial(kernel, L, Z, side), out_shape=(state, s...]
    all_gather x1 -> x0, waiting for transfers between devices: 46.5 us -> none  [local(): lax.all_gather(coarse_terms[None], 'layer', axis=0, tiled=True)]
    psum x1 -> x0, waiting for transfers between devices: 42.4 us -> none  [local(): summed_grad = lax.psum(gradients, 'dp')]
    ppermute x4 -> x0, starting transfers between devices: 14.3 us -> none  [shifted(): return lax.ppermute(block, axis, route)]
    unnamed x76 -> x12, local copies, waits for them, and re-layouts: 21.1 us -> 6.89 us
    psum x1 -> x0, blocking collectives: 13.8 us -> none  [local(): squares = lax.psum(jnp.sum(summed_grad * summed_grad), 'layer')]
    dot_general x8 -> x0, matrix products: 11.5 us -> none  [the longest x4 5.81 us: conv_apply(): jnp.dot(columns, kernel_set.reshape(9 * channels, channels), preferred_el...]
    dot_general x1 -> x0, local copies, waits for them, and re-layouts: 4.28 us -> none  [conv_weight(): lax.dot_general(columns, flat_error, (((0,), (0,)), ((), ())), preferred_...]
  transfers between devices with their start and end apart: 6 -> 0, of which waited for: 4 -> 0; matrix products, arithmetic and copies ran while one was open for 9% -> 0% of each run, Pallas kernels for 0% -> 0%
where the time goes in v1:
time: 83 us; the launch traced here: 82.7 us
  Pallas kernels  73 us (88%)
  local copies, waits for them, and re-layouts  6.89 us (8%)
  other arithmetic  1.47 us (2%)
  between operations  1.35 us (2%)
    pallas_call x1, Pallas kernels, local(): pl.pallas_call(functools.partial(kernel, L, Z, side), out_shape=(state, s...  73 us
    unnamed x12, local copies, waits for them, and re-layouts  6.89 us

profile of v1, /device:TPU:0, one launch (start us, length us, event | category | flops | bytes accessed | tf_op | source)
XLA Modules:
  0.0 82.7 jit_solution(7635529075276782891)
XLA Ops:
  0.6 0.0 copy-start.3
  0.6 0.7 copy-done.3
  1.3 0.0 copy-start
  1.3 1.0 %copy-done = f32[1,1,32,32,128]{4,3,2,1,0:T(8,128)S(1)} copy-done((f32[1,1,32,32,128]{4,3,2,1,0:T(8,128)S(1)}, f32[1,1,32,32,128]{4,3,2,1,0:T(8,128)}, u32[]{:S(2)}) %copy-start) | copy-done | bytes 524312
  2.4 0.0 copy-start.1
  2.4 1.0 %copy-done.1 = f32[1,1,32,32,128]{4,3,2,1,0:T(8,128)S(1)} copy-done((f32[1,1,32,32,128]{4,3,2,1,0:T(8,128)S(1)}, f32[1,1,32,32,128]{4,3,2,1,0:T(8,128)}, u32[]{:S(2)}) %copy-start.1) | copy-done | bytes 524312
  3.4 0.0 copy-start.2
  3.4 1.0 %copy-done.2 = bf16[1,9,128,128]{3,2,1,0:T(8,128)(2,1)S(1)} copy-done((bf16[1,9,128,128]{3,2,1,0:T(8,128)(2,1)S(1)}, bf16[1,9,128,128]{3,2,1,0:T(8,128)(2,1)}, u32[]{:S(2)}) %copy-start.2) | copy-done | bytes 294936
  4.4 73.0 %shard_map.83 = (f32[1024,128]{1,0:T(8,128)S(1)}, f32[1024,128]{1,0:T(8,128)S(1)}, f32[9,128,128]{2,1,0:T(8,128)S(1)}, f32[8,128]{1,0:T(8,128)S(1)}, f32[1024,128]{1,0:T(8,128)S(1)}, /*index=5*/f32[1024,128]{1,0:T(8,128)S(1)}) custom-call(f32[1024,128]{1,0:T(8,128)S(1)} %bitcast.13, bf16[3,384,128]{2,1,0:T(8,128)(2,1)S(1)} %bitcast.15, ...), custom_call_target="tpu_custom_call" | custom-call | tf_op jit(solution)/shard_map/pallas_call | solution.py:293
  77.4 0.6 reduce_sum.9
  78.7 0.9 %divide_bitcast_fusion = f32[1,9,128,128]{3,2,1,0:T(8,128)} fusion(f32[9,128,128]{2,1,0:T(8,128)S(1)} %get-tuple-element.13, f32[]{:T(128)S(6)} %sqrt.3), kind=kLoop, calls=%fused_computation | loop fusion | flops 147456 | bytes 1179652 | tf_op jit(solution)/shard_map/reshape | solution.py:320
  79.5 0.8 copy.13
  80.3 0.8 copy.14
  81.1 0.8 copy.15
  81.9 0.8 copy.16
Async XLA Ops:
  0.6 0.7 copy-start.3
  1.3 1.0 %copy-start = (f32[1,1,32,32,128]{4,3,2,1,0:T(8,128)S(1)}, f32[1,1,32,32,128]{4,3,2,1,0:T(8,128)}, u32[]{:S(2)}) copy-start(f32[1,1,32,32,128]{4,3,2,1,0:T(8,128)} %param.4) | copy-start | bytes 1572868
  2.4 1.0 %copy-start.1 = (f32[1,1,32,32,128]{4,3,2,1,0:T(8,128)S(1)}, f32[1,1,32,32,128]{4,3,2,1,0:T(8,128)}, u32[]{:S(2)}) copy-start(f32[1,1,32,32,128]{4,3,2,1,0:T(8,128)} %param.6) | copy-start | bytes 1572868
  3.4 1.0 %copy-start.2 = (bf16[1,9,128,128]{3,2,1,0:T(8,128)(2,1)S(1)}, bf16[1,9,128,128]{3,2,1,0:T(8,128)(2,1)}, u32[]{:S(2)}) copy-start(bf16[1,9,128,128]{3,2,1,0:T(8,128)(2,1)} %param.5) | copy-start | bytes 884740

commit v2 on v1

--- a/solution.py
+++ b/solution.py
@@ -13,11 +13,25 @@
 
 
 def kernel(
-    L, Z, side, anchor, kern, aend, gain,
-    ns, ast, gsum, sqsum, rc, ac,
-    tx, rx, off, xcf, xcd, slopes, xt, wb, gacc, gout_rx, gin_rx, sqrx, sqtx,
-    send_sem, recv_sem, gsend_in, grecv_out, gsend_out, grecv_in, sq_send, sq_recv,
+    L, Z, side, anchor_hbm, kern_hbm, aend_hbm, gain,
+    ns_hbm, ast_hbm, gsum_hbm, sqsum, rc_hbm, ac_hbm,
+    ns, ast, gsum, rc, ac, anchor, kern, aend, tx, rx, off, off_rx,  xcf, xcd, slopes, xt, wb, gacc, gout_rx, gin_rx, sqrx, sqtx,
+    in_sem, out_sem, gout_sem, send_sem, recv_sem, off_send, off_recv, relay_sem, gsend_in, grecv_out, gsend_out, grecv_in, sq_send, sq_recv,
 ):
+    loads = [
+        pltpu.make_async_copy(a, b, in_sem.at[i])
+        for i, (a, b) in enumerate(((anchor_hbm, anchor), (kern_hbm, kern), (aend_hbm, aend)))
+    ]
+    for load in loads:
+        load.start()
+    stores = [
+        pltpu.make_async_copy(a, b, out_sem.at[i])
+        for i, (a, b) in enumerate(((ns, ns_hbm), (ast, ast_hbm), (rc, rc_hbm), (ac, ac_hbm)))
+    ]
+
+    def gstore(t):
+        return pltpu.make_async_copy(gsum.at[t], gsum_hbm.at[t], gout_sem.at[t])
+
     n, ch = anchor.shape
     nc = CHUNKS
     R = n // nc
@@ -62,24 +76,42 @@
 
     up = lax.rem(pos + 1, L)
     down = lax.rem(pos + L - 1, L)
+    odd = lax.rem(pos, 2) == 1
+    ahead = jnp.where(odd, lax.rem(pos + 2, L), up)
+    paired_even = (pos >= 4) & (lax.rem(pos, 2) == 0)
+    paired_odd = (pos >= 5) & odd
+    target = (up, up, ahead, down, down)
+    sends = (
+        not_last,
+        (pos > 0) & (pos < L - 1),
+        (pos == 2) | ((pos >= 3) & (pos < L - 2) & odd),
+        not_first,
+        (pos > 0) & (pos < L - 1),
+    )
+    gets = (not_first, pos > 1, pos > 2, not_last, pos < L - 2)
 
     def send(phase, c):
-        if phase < 3:
-            pl.when(not_last)(lambda: link(phase, c, up).start())
-        else:
-            pl.when(not_first)(lambda: link(phase, c, down).start())
+        pl.when(sends[phase])(lambda: link(phase, c, target[phase]).start())
 
     def arrive(phase, c):
-        if phase < 3:
-            pl.when(not_first)(lambda: link(phase, c, up).wait_recv())
-        else:
-            pl.when(not_last)(lambda: link(phase, c, down).wait_recv())
+        pl.when(gets[phase])(lambda: link(phase, c, target[phase]).wait_recv())
 
     def sent(phase, c):
-        if phase < 3:
-            pl.when(not_last)(lambda: link(phase, c, up).wait_send())
-        else:
-            pl.when(not_first)(lambda: link(phase, c, down).wait_send())
+        pl.when(sends[phase])(lambda: link(phase, c, target[phase]).wait_send())
+
+    def off_link(c):
+        return pltpu.make_async_remote_copy(
+            src_ref=off.at[rows(c)], dst_ref=off_rx.at[rows(c)], send_sem=off_send.at[c],
+            recv_sem=off_recv.at[c], device_id={"layer": up},
+            device_id_type=pl.DeviceIdType.MESH,
+        )
+
+    def relay(c):
+        return pltpu.make_async_remote_copy(
+            src_ref=rx.at[2, rows(c)], dst_ref=rx.at[2, rows(c)], send_sem=relay_sem.at[c],
+            recv_sem=recv_sem.at[2, c], device_id={"layer": down},
+            device_id_type=pl.DeviceIdType.MESH,
+        )
 
     across = lax.broadcasted_iota(jnp.int32, (R, ch), 0) % side
     left_ok = across > 0
@@ -105,6 +137,8 @@
         xc[0:side, :] = zeros
         xc[n + side : n + 2 * side, :] = zeros
 
+    loads[0].wait()
+    loads[1].wait()
     for c in range(nc):
         stage(xcf, c, anchor[rows(c), :])
     for c in range(nc):
@@ -115,8 +149,10 @@
 
     @pl.when(is_first)
     def _():
-        for p in range(3):
+        for p in range(2):
             rx[p] = anchor[...]
+
+    loads[2].wait()
 
     @pl.when(is_last)
     def _():
@@ -129,6 +165,7 @@
             wb[d, e * ch : (e + 1) * ch, :] = tap.astype(jnp.float32).T.astype(jnp.bfloat16)
 
     block_gain = gain[pl.ds(pos, 1), :]
+    before_gain = gain[pl.ds(jnp.maximum(pos - 1, 0), 1), :]
 
     def second(c):
         tx[1, rows(c), :] = rx[0, rows(c), :] + h * jnp.tanh(conv(xcf, kern, c))
@@ -137,6 +174,11 @@
     for c in range(nc):
         arrive(0, c)
         stage(xcf, c, rx[0, rows(c), :])
+
+        @pl.when(pos == 1)
+        def _():
+            rx[1, rows(c), :] = rx[0, rows(c), :]
+
         if c > 0:
             second(c - 1)
     second(nc - 1)
@@ -146,6 +188,7 @@
         end = start + h * jnp.tanh(conv(xcf, kern, c))
         rc[rows(c), :] = end - tx[1, rows(c), :]
         off[rows(c), :] = end - block_gain * start
+        pl.when(paired_even)(lambda: off_link(c).start())
 
     for c in range(nc):
         arrive(1, c)
@@ -153,6 +196,7 @@
         if c > 0:
             third(c - 1)
     third(nc - 1)
+    stores[2].start()
 
     def record(c):
         act = jnp.tanh(conv(xcf, kern, c))
@@ -161,14 +205,29 @@
 
     for c in range(nc):
         arrive(2, c)
-        state = rx[2, rows(c), :]
+
+        @pl.when(pos <= 2)
+        def _():
+            ns[rows(c), :] = rx[1, rows(c), :]
+
+        @pl.when((pos == 3) | paired_even)
+        def _():
+            ns[rows(c), :] = rx[2, rows(c), :]
+
+        @pl.when(paired_odd)
+        def _():
+            relay(c).start()
+            off_link(c).wait_recv()
+            ns[rows(c), :] = before_gain * rx[2, rows(c), :] + off_rx[rows(c), :]
+
+        state = ns[rows(c), :]
         tx[2, rows(c), :] = block_gain * state + off[rows(c), :]
         send(2, c)
-        ns[rows(c), :] = state
         stage(xcf, c, state)
         if c > 0:
             record(c - 1)
     record(nc - 1)
+    stores[0].start()
 
     for c in range(nc):
         stage(xcd, c, aend[rows(c), :] * slopes[rows(c), :])
@@ -183,6 +242,11 @@
     for c in range(nc):
         arrive(3, c)
         stage(xcd, c, rx[3, rows(c), :] * slopes[rows(c), :])
+
+        @pl.when(pos == L - 2)
+        def _():
+            rx[4, rows(c), :] = rx[3, rows(c), :]
+
         if c > 0:
             second_back(c - 1)
     second_back(nc - 1)
@@ -239,6 +303,7 @@
             gsum[t] = gin_rx[t]
 
         pl.when(has_out)(lambda: g_out(t).start())
+        gstore(t).start()
 
     def finish(c):
         done = rx[4, rows(c), :] + h * conv(xcd, wb, c)
@@ -251,6 +316,9 @@
             towards(t)
         if t < nc:
             finish(t)
+        if t == nc:
+            stores[1].start()
+            stores[3].start()
         if t >= LAG:
             outwards(t - LAG)
             block = gsum[t - LAG]
@@ -270,15 +338,43 @@
     for p in range(5):
         for c in range(nc):
             sent(p, c)
+    for c in range(nc):
+        pl.when(paired_even)(lambda c=c: off_link(c).wait_send())
+        pl.when(paired_odd)(lambda c=c: relay(c).wait_send())
     for t in range(9):
         g_in(t, gin_rx).wait_send()
+        gstore(t).wait()
         pl.when(has_out)(lambda t=t: g_out(t).wait_send())
+    for store in stores:
+        store.wait()
     for k in range(1, L):
         sq(k).wait_recv()
         squares = squares + sqrx[k - 1]
     sqsum[...] = squares
     for k in range(1, L):
         sq(k).wait_send()
+
+
+def write_out(
+    entries, ns, ast, gsum, sq, rc, ac, ns_hbm, ast_hbm, wg_hbm, rc_hbm, ac_hbm, g, wg, sem, gsem, wsem
+):
+    load = pltpu.make_async_copy(gsum, g, gsem)
+    load.start()
+    pairs = ((ns, ns_hbm), (ast, ast_hbm), (rc, rc_hbm), (ac, ac_hbm))
+    copies = [pltpu.make_async_copy(a, b, sem.at[i]) for i, (a, b) in enumerate(pairs)]
+    for copy in copies:
+        copy.start()
+    mean = jnp.sum(sq[...], keepdims=True) / entries
+    root = jnp.sqrt(mean + EPSILON)
+    load.wait()
+    for d in range(3):
+        at = pl.ds(3 * d, 3)
+        wg[at] = g[at] / root[None]
+        copy = pltpu.make_async_copy(wg.at[at], wg_hbm.at[at], wsem.at[d])
+        copy.start()
+        copies.append(copy)
+    for copy in copies:
+        copy.wait()
 
 
 def local(L, Z, states_guess, kernels, adjoint_end, coarse_gain):
@@ -288,6 +384,7 @@
     f32, bf16 = jnp.float32, jnp.bfloat16
     state = jax.ShapeDtypeStruct((n, ch), f32)
     vm = pl.BlockSpec(memory_space=pltpu.VMEM)
+    hbm = pl.BlockSpec(memory_space=pltpu.HBM)
     V = pltpu.VMEM
     D = pltpu.SemaphoreType.DMA
     ns, ast, gsum, sq, rc, ac = pl.pallas_call(
@@ -296,25 +393,34 @@
             state, state, jax.ShapeDtypeStruct((9, ch, ch), f32),
             jax.ShapeDtypeStruct((8, ch), f32), state, state,
         ),
-        in_specs=[vm] * 4,
-        out_specs=(vm,) * 6,
+        in_specs=[hbm] * 3 + [vm],
+        out_specs=(hbm, hbm, hbm, vm, hbm, hbm),
         scratch_shapes=[
-            V((5, n, ch), f32), V((5, n, ch), f32), V((n, ch), f32),
+            V((n, ch), f32), V((n, ch), f32), V((9, ch, ch), f32), V((n, ch), f32), V((n, ch), f32),
+            V((n, ch), f32), V((3, 3 * ch, ch), bf16), V((n, ch), f32),
+            V((5, n, ch), f32), V((5, n, ch), f32), V((n, ch), f32), V((n, ch), f32),
             V((n + 2 * side, 3 * ch), bf16), V((n + 2 * side, 3 * ch), bf16),
             V((n, ch), f32), V((3 * ch, n), bf16), V((3, 3 * ch, ch), bf16),
             V((9, ch, ch), f32), V((9, ch, ch), f32), V((9, ch, ch), f32),
             V((L - 1, 8, ch), f32), V((8, ch), f32),
-            D((5, CHUNKS)), D((5, CHUNKS)), D((9,)), D((9,)), D((9,)), D((9,)),
+            D((3,)), D((4,)), D((9,)), D((5, CHUNKS)), D((5, CHUNKS)), D((CHUNKS,)), D((CHUNKS,)), D((CHUNKS,)), D((9,)), D((9,)), D((9,)), D((9,)),
             D((L - 1,)), D((L - 1,)),
         ],
         compiler_params=pltpu.CompilerParams(
-            collective_id=0, has_side_effects=True, vmem_limit_bytes=48 * 1024 * 1024
+            collective_id=0, has_side_effects=True, vmem_limit_bytes=62 * 1024 * 1024
         ),
     )(
         states_guess.reshape(n, ch), kernels.reshape(3, 3 * ch, ch),
         adjoint_end.reshape(n, ch), coarse_gain,
     )
-    weight_grad = gsum / jnp.sqrt(jnp.sum(sq) / (L * 9 * ch * ch) + EPSILON)
+    ns, ast, weight_grad, rc, ac = pl.pallas_call(
+        functools.partial(write_out, L * 9 * ch * ch),
+        out_shape=(state, state, jax.ShapeDtypeStruct((9, ch, ch), f32), state, state),
+        in_specs=[hbm, hbm, hbm, vm, hbm, hbm],
+        out_specs=(hbm,) * 5,
+        scratch_shapes=[V((9, ch, ch), f32), V((9, ch, ch), f32), D((4,)), D, D((3,))],
+        compiler_params=pltpu.CompilerParams(vmem_limit_bytes=62 * 1024 * 1024),
+    )(ns, ast, gsum, sq, rc, ac)
     full = states_guess.shape
     return (
         ns.reshape(full), ast.reshape(full), weight_grad.reshape(1, 9, ch, ch),

time: 83 us -> 141 us (1.70)
  Pallas kernels: 73 us -> 141 us
  local copies, waits for them, and re-layouts: 6.89 us -> 0 us
  other arithmetic: 1.47 us -> 0 us
    pallas_call x0 -> x1, Pallas kernels: none -> 65.4 us  [local(): pl.pallas_call(functools.partial(write_out, L * 9 * ch * ch), out_shape=(...]
    unnamed x12 -> x0, local copies, waits for them, and re-layouts: 6.89 us -> none
    pallas_call x1, Pallas kernels: 73 us -> 75.1 us  [local(): pl.pallas_call(functools.partial(kernel, L, Z, side), out_shape=(state, s...]
where the time goes in v2:
time: 141 us
  Pallas kernels  141 us (100%)
    pallas_call x1, Pallas kernels, local(): pl.pallas_call(functools.partial(kernel, L, Z, side), out_shape=(state, s...  75.1 us
    pallas_call x1, Pallas kernels, local(): pl.pallas_call(functools.partial(write_out, L * 9 * ch * ch), out_shape=(...  65.4 us

profile of v2, /device:TPU:0, one launch (start us, length us, event | category | flops | bytes accessed | tf_op | source)
XLA Modules:
  0.0 141.2 jit_solution(4376041135475403353)
XLA Ops:
  0.6 75.1 %shard_map.83 = (f32[1024,128]{1,0:T(8,128)}, f32[1024,128]{1,0:T(8,128)}, f32[9,128,128]{2,1,0:T(8,128)}, f32[8,128]{1,0:T(8,128)}, f32[1024,128]{1,0:T(8,128)}, /*index=5*/f32[1024,128]{1,0:T(8,128)}) custom-call(f32[1024,128]{1,0:T(8,128)} %bitcast.8, bf16[3,384,128]{2,1,0:T(8,128)(2,1)} %bitcast.10, f32[1024,128]{1,0:T(8,128)} %bitcast.9, f32[8,128]{1,0:T(8,128)} %gain.1), custom_call_target="tpu_custom_call" | custom-call | tf_op jit(solution)/shard_map/pallas_call | solution.py:390
  75.8 65.4 %shard_map.84 = (f32[1024,128]{1,0:T(8,128)}, f32[1024,128]{1,0:T(8,128)}, f32[9,128,128]{2,1,0:T(8,128)}, f32[1024,128]{1,0:T(8,128)}, f32[1024,128]{1,0:T(8,128)}) custom-call(f32[1024,128]{1,0:T(8,128)} %get-tuple-element.16.ns, f32[1024,128]{1,0:T(8,128)} %get-tuple-element.17.ast, f32[9,128,128]{2,1,0:T(8,128)} %get-tuple-element.18.gsum, ...), custom_call_target="tpu_custom_call" | custom-call | tf_op jit(solution)/shard_map/pallas_call | solution.py:416

commit v3 on v2

--- a/solution.py
+++ b/solution.py
@@ -8,8 +8,9 @@
 from jax.sharding import PartitionSpec as P
 
 EPSILON = 1e-06
-CHUNKS = 4
-LAG = 2
+CHUNKS = 8
+LAG = 3
+PIECES = 18
 
 
 def kernel(
@@ -277,11 +278,13 @@
         three = h * jnp.dot(
             xt[...], xcd[pl.ds((2 - d) * side, n), ch : 2 * ch], preferred_element_type=jnp.float32
         )
-        for e in range(3):
-            gacc[3 * d + e] = three[e * ch : (e + 1) * ch, :]
+        each = PIECES // 3
+        deep = 3 * ch // each
+        for e in range(each):
+            gacc[each * d + e] = three[e * deep : (e + 1) * deep, :]
 
             @pl.when(no_out)
-            def _(t=3 * d + e):
+            def _(t=each * d + e):
                 push(t)
 
     def towards(t):
@@ -311,8 +314,8 @@
         ac[rows(c), :] = done - tx[4, rows(c), :]
 
     squares = jnp.zeros((8, ch), jnp.float32)
-    for t in range(9 + LAG):
-        if t < 9:
+    for t in range(PIECES + LAG):
+        if t < PIECES:
             towards(t)
         if t < nc:
             finish(t)
@@ -322,7 +325,7 @@
         if t >= LAG:
             outwards(t - LAG)
             block = gsum[t - LAG]
-            squares = squares + jnp.sum((block * block).reshape(ch // 8, 8, ch), axis=0)
+            squares = squares + jnp.sum((block * block).reshape(-1, 8, ch), axis=0)
 
     sqtx[...] = squares
 
@@ -341,7 +344,7 @@
     for c in range(nc):
         pl.when(paired_even)(lambda c=c: off_link(c).wait_send())
         pl.when(paired_odd)(lambda c=c: relay(c).wait_send())
-    for t in range(9):
+    for t in range(PIECES):
         g_in(t, gin_rx).wait_send()
         gstore(t).wait()
         pl.when(has_out)(lambda t=t: g_out(t).wait_send())
@@ -356,23 +359,28 @@
 
 
 def write_out(
-    entries, ns, ast, gsum, sq, rc, ac, ns_hbm, ast_hbm, wg_hbm, rc_hbm, ac_hbm, g, wg, sem, gsem, wsem
+    entries, ns, ast, gsum, sq, rc, ac, ns_hbm, ast_hbm, wg_hbm, rc_hbm, ac_hbm,
+    held, g, wg, in_sem, sem, gsem, wsem,
 ):
-    load = pltpu.make_async_copy(gsum, g, gsem)
-    load.start()
     pairs = ((ns, ns_hbm), (ast, ast_hbm), (rc, rc_hbm), (ac, ac_hbm))
-    copies = [pltpu.make_async_copy(a, b, sem.at[i]) for i, (a, b) in enumerate(pairs)]
-    for copy in copies:
-        copy.start()
+    loads = [pltpu.make_async_copy(a, held.at[i], in_sem.at[i]) for i, (a, b) in enumerate(pairs)]
+    copies = [pltpu.make_async_copy(held.at[i], b, sem.at[i]) for i, (a, b) in enumerate(pairs)]
+    first = pltpu.make_async_copy(gsum, g, gsem)
+    first.start()
+    for load in loads:
+        load.start()
     mean = jnp.sum(sq[...], keepdims=True) / entries
     root = jnp.sqrt(mean + EPSILON)
-    load.wait()
+    first.wait()
     for d in range(3):
         at = pl.ds(3 * d, 3)
         wg[at] = g[at] / root[None]
         copy = pltpu.make_async_copy(wg.at[at], wg_hbm.at[at], wsem.at[d])
         copy.start()
         copies.append(copy)
+    for load, copy in zip(loads, copies[:4]):
+        load.wait()
+        copy.start()
     for copy in copies:
         copy.wait()
 
@@ -383,6 +391,7 @@
     n = images * side * side
     f32, bf16 = jnp.float32, jnp.bfloat16
     state = jax.ShapeDtypeStruct((n, ch), f32)
+    parts = (PIECES, 9 * ch // PIECES, ch)
     vm = pl.BlockSpec(memory_space=pltpu.VMEM)
     hbm = pl.BlockSpec(memory_space=pltpu.HBM)
     V = pltpu.VMEM
@@ -390,20 +399,20 @@
     ns, ast, gsum, sq, rc, ac = pl.pallas_call(
         functools.partial(kernel, L, Z, side),
         out_shape=(
-            state, state, jax.ShapeDtypeStruct((9, ch, ch), f32),
+            state, state, jax.ShapeDtypeStruct(parts, f32),
             jax.ShapeDtypeStruct((8, ch), f32), state, state,
         ),
         in_specs=[hbm] * 3 + [vm],
         out_specs=(hbm, hbm, hbm, vm, hbm, hbm),
         scratch_shapes=[
-            V((n, ch), f32), V((n, ch), f32), V((9, ch, ch), f32), V((n, ch), f32), V((n, ch), f32),
+            V((n, ch), f32), V((n, ch), f32), V(parts, f32), V((n, ch), f32), V((n, ch), f32),
             V((n, ch), f32), V((3, 3 * ch, ch), bf16), V((n, ch), f32),
             V((5, n, ch), f32), V((5, n, ch), f32), V((n, ch), f32), V((n, ch), f32),
             V((n + 2 * side, 3 * ch), bf16), V((n + 2 * side, 3 * ch), bf16),
             V((n, ch), f32), V((3 * ch, n), bf16), V((3, 3 * ch, ch), bf16),
-            V((9, ch, ch), f32), V((9, ch, ch), f32), V((9, ch, ch), f32),
+            V(parts, f32), V(parts, f32), V(parts, f32),
             V((L - 1, 8, ch), f32), V((8, ch), f32),
-            D((3,)), D((4,)), D((9,)), D((5, CHUNKS)), D((5, CHUNKS)), D((CHUNKS,)), D((CHUNKS,)), D((CHUNKS,)), D((9,)), D((9,)), D((9,)), D((9,)),
+            D((3,)), D((4,)), D((PIECES,)), D((5, CHUNKS)), D((5, CHUNKS)), D((CHUNKS,)), D((CHUNKS,)), D((CHUNKS,)), D((PIECES,)), D((PIECES,)), D((PIECES,)), D((PIECES,)),
             D((L - 1,)), D((L - 1,)),
         ],
         compiler_params=pltpu.CompilerParams(
@@ -418,9 +427,12 @@
         out_shape=(state, state, jax.ShapeDtypeStruct((9, ch, ch), f32), state, state),
         in_specs=[hbm, hbm, hbm, vm, hbm, hbm],
         out_specs=(hbm,) * 5,
-        scratch_shapes=[V((9, ch, ch), f32), V((9, ch, ch), f32), D((4,)), D, D((3,))],
+        scratch_shapes=[
+            V((4, n, ch), f32), V((9, ch, ch), f32), V((9, ch, ch), f32),
+            D((4,)), D((4,)), D, D((3,)),
+        ],
         compiler_params=pltpu.CompilerParams(vmem_limit_bytes=62 * 1024 * 1024),
-    )(ns, ast, gsum, sq, rc, ac)
+    )(ns, ast, gsum.reshape(9, ch, ch), sq, rc, ac)
     full = states_guess.shape
     return (
         ns.reshape(full), ast.reshape(full), weight_grad.reshape(1, 9, ch, ch),

time: 141 us -> 78.8 us (0.56)
  Pallas kernels: 141 us -> 77.9 us
    pallas_call x1, Pallas kernels: 65.4 us -> 3.86 us  [local(): pl.pallas_call(functools.partial(write_out, L * 9 * ch * ch), out_shape=(...]
where the time goes in v3:
time: 78.8 us; the launch traced here: 78.6 us
  Pallas kernels  77.9 us (99%)
    pallas_call x1, Pallas kernels, local(): pl.pallas_call(functools.partial(kernel, L, Z, side), out_shape=(state, s...  74.1 us
    pallas_call x1, Pallas kernels, local(): pl.pallas_call(functools.partial(write_out, L * 9 * ch * ch), out_shape=(...  3.86 us

profile of v3, /device:TPU:0, one launch (start us, length us, event | category | flops | bytes accessed | tf_op | source)
XLA Modules:
  0.0 78.6 jit_solution(14505482420655240211)
XLA Ops:
  0.6 74.1 %shard_map.83 = (f32[1024,128]{1,0:T(8,128)}, f32[1024,128]{1,0:T(8,128)}, f32[18,64,128]{2,1,0:T(8,128)}, f32[8,128]{1,0:T(8,128)}, f32[1024,128]{1,0:T(8,128)}, /*index=5*/f32[1024,128]{1,0:T(8,128)}) custom-call(f32[1024,128]{1,0:T(8,128)} %bitcast.10, bf16[3,384,128]{2,1,0:T(8,128)(2,1)} %bitcast.12, f32[1024,128]{1,0:T(8,128)} %bitcast.11, f32[8,128]{1,0:T(8,128)} %gain.1), custom_call_target="tpu_custom_call" | custom-call | tf_op jit(solution)/shard_map/pallas_call | solution.py:399
  74.7 3.9 %shard_map.84 = (f32[1024,128]{1,0:T(8,128)}, f32[1024,128]{1,0:T(8,128)}, f32[9,128,128]{2,1,0:T(8,128)}, f32[1024,128]{1,0:T(8,128)}, f32[1024,128]{1,0:T(8,128)}) custom-call(f32[1024,128]{1,0:T(8,128)} %get-tuple-element.16.ns, f32[1024,128]{1,0:T(8,128)} %get-tuple-element.17.ast, f32[9,128,128]{2,1,0:T(8,128)} %bitcast.9, ...), custom_call_target="tpu_custom_call" | custom-call | tf_op jit(solution)/shard_map/pallas_call | solution.py:425

commit v4 on v3

--- a/solution.py
+++ b/solution.py
@@ -202,7 +202,6 @@
     def record(c):
         act = jnp.tanh(conv(xcf, kern, c))
         slopes[rows(c), :] = 1.0 - act * act
-        xt[:, rows(c)] = xcf[pl.ds(side + c * R, R), :].T
 
     for c in range(nc):
         arrive(2, c)
@@ -235,6 +234,8 @@
     for c in range(nc):
         tx[3, rows(c), :] = aend[rows(c), :] + h * conv(xcd, wb, c)
         send(3, c)
+    for c in range(nc):
+        xt[:, rows(c)] = xcf[pl.ds(side + c * R, R), :].T
 
     def second_back(c):
         tx[4, rows(c), :] = rx[3, rows(c), :] + h * conv(xcd, wb, c)

time: 78.8 us -> 78.8 us (level)
  no operation moved by 1% of the time
where the time goes in v4:
time: 78.8 us; the launch traced here: 78.6 us
  Pallas kernels  77.9 us (99%)
    pallas_call x1, Pallas kernels, local(): pl.pallas_call(functools.partial(kernel, L, Z, side), out_shape=(state, s...  74.1 us
    pallas_call x1, Pallas kernels, local(): pl.pallas_call(functools.partial(write_out, L * 9 * ch * ch), out_shape=(...  3.86 us

profile of v4, /device:TPU:0, one launch (start us, length us, event | category | flops | bytes accessed | tf_op | source)
XLA Modules:
  0.0 78.6 jit_solution(18166502873746110902)
XLA Ops:
  0.6 74.1 %shard_map.83 = (f32[1024,128]{1,0:T(8,128)}, f32[1024,128]{1,0:T(8,128)}, f32[18,64,128]{2,1,0:T(8,128)}, f32[8,128]{1,0:T(8,128)}, f32[1024,128]{1,0:T(8,128)}, /*index=5*/f32[1024,128]{1,0:T(8,128)}) custom-call(f32[1024,128]{1,0:T(8,128)} %bitcast.10, bf16[3,384,128]{2,1,0:T(8,128)(2,1)} %bitcast.12, f32[1024,128]{1,0:T(8,128)} %bitcast.11, f32[8,128]{1,0:T(8,128)} %gain.1), custom_call_target="tpu_custom_call" | custom-call | tf_op jit(solution)/shard_map/pallas_call | solution.py:400
  74.7 3.9 %shard_map.84 = (f32[1024,128]{1,0:T(8,128)}, f32[1024,128]{1,0:T(8,128)}, f32[9,128,128]{2,1,0:T(8,128)}, f32[1024,128]{1,0:T(8,128)}, f32[1024,128]{1,0:T(8,128)}) custom-call(f32[1024,128]{1,0:T(8,128)} %get-tuple-element.16.ns, f32[1024,128]{1,0:T(8,128)} %get-tuple-element.17.ast, f32[9,128,128]{2,1,0:T(8,128)} %bitcast.9, ...), custom_call_target="tpu_custom_call" | custom-call | tf_op jit(solution)/shard_map/pallas_call | solution.py:426
